TPU v7x, 32 devices: a whole 2x2x4 slice. The times are simulated.
32 devices in a mesh: groups: 2 (over x), wide: 16 (over z, y, core).
Axes of the slice: x: 2, y: 2, z: 4, core: 2. Of those that a mesh axis runs over, the one named last changes fastest.
Arguments:
- picture_feature_maps: bfloat16 [256, 10, 10, 1536], P(('groups', 'wide')), parts along dimension 0, may hold values from -6 to 6
- partitioned_filter_tensor: bfloat16 [3, 3, 128, 1536], replicated, may hold values from -0.1875 to 0.1875
- picture_token_layer_scaling: float32 [1536], replicated, may hold values from 0.1 to 1.9
- summary_probes: bfloat16 [64, 1536], replicated, may hold values from -6 to 6
- summary_probe_layer_scaling: float32 [1536], replicated, may hold values from 0.1 to 1.9
- asking_projection_tensor: bfloat16 [1536, 1536], P('wide'), may hold values from -0.15625 to 0.15625
- lookup_projection_tensor: bfloat16 [1536, 1536], P('wide'), may hold values from -0.15625 to 0.15625
- content_projection_tensor: bfloat16 [1536, 1536], P('wide'), may hold values from -0.15625 to 0.15625
- final_projection_tensor: bfloat16 [1536, 1536], P(None, 'wide'), may hold values from -0.15625 to 0.15625
- sharpness_coefficient: float32 [16], replicated, may hold values from 0.5 to 64
Outputs:
- attended: float32 [128, 1536], P('groups'), parts along dimension 0
- new_latents: bfloat16 [128, 1536], P('groups'), parts along dimension 0
There are 2 independent parts, one for each index of `groups`. A program takes and returns all parts, laid end to end along the dimension named above; an argument that names none is the same for every part. Nothing has to cross between parts.
All inputs are finite; a program needn't handle non-finite values.
Results may differ from a plain program's by a relative error of at most 0.004.
The roundings to bfloat16 on the way count: a program that leaves them out, or rounds other values in their place, can miss the bound.
Values may be sent and summed in bfloat16 or wider, within the bound.
A program may use at most 128 MiB of HBM per device.

v0:
```python
import math
import jax
import jax.numpy as jnp
from jax import lax
from jax.sharding import PartitionSpec as P

RESIDUAL_SCALE = 0.2
EPSILON = 1e-06


def layer_norm(values, gain):
    center = values - jnp.mean(values, axis=-1, keepdims=True)
    spread = jnp.mean(center * center, axis=-1, keepdims=True)
    return center * lax.rsqrt(spread + EPSILON) * gain


def combine(left_side, right_side):
    left_max, left_sum, left_weighted = left_side
    right_max, right_sum, right_weighted = right_side
    joint_max = jnp.maximum(left_max, right_max)
    scale_left = jnp.exp(left_max - joint_max)
    scale_right = jnp.exp(right_max - joint_max)
    return (
        joint_max,
        left_sum * scale_left + right_sum * scale_right,
        left_weighted * scale_left[..., None] + right_weighted * scale_right[..., None],
    )


def merge_all(row_max, row_sum, weighted):
    joint_max = lax.pmax(row_max, "wide")
    factor = jnp.exp(row_max - joint_max)
    joint_sum, joint_weighted = lax.psum((row_sum * factor, weighted * factor[..., None]), "wide")
    return (joint_max, joint_sum, joint_weighted)


def softmax_terms(scores, carried):
    row_max = jnp.max(scores, axis=-1)
    weights = jnp.exp(scores - row_max[..., None])
    row_sum = jnp.sum(weights, axis=-1)
    weighted = jnp.einsum("hlt,thd->hld", weights, carried, precision=lax.Precision.HIGHEST)
    return (row_max, row_sum, weighted)


def per_device(
    picture_feature_maps,
    partitioned_filter_tensor,
    picture_token_layer_scaling,
    summary_probes,
    summary_probe_layer_scaling,
    asking_projection_tensor,
    lookup_projection_tensor,
    content_projection_tensor,
    final_projection_tensor,
    sharpness_coefficient,
):
    channels = picture_feature_maps.shape[3]
    subspace_number_overall = sharpness_coefficient.shape[0]
    subspace_breadth = channels // subspace_number_overall
    lat_count = summary_probes.shape[0]
    activated = jax.nn.gelu(picture_feature_maps.astype(jnp.float32)).astype(jnp.bfloat16)
    convolved = lax.conv_general_dilated(
        activated,
        partitioned_filter_tensor,
        (1, 1),
        "SAME",
        dimension_numbers=("NHWC", "HWIO", "NHWC"),
        feature_group_count=channels // partitioned_filter_tensor.shape[2],
        preferred_element_type=jnp.float32,
    )
    summed = picture_feature_maps.astype(jnp.float32) + RESIDUAL_SCALE * convolved
    tok_norm = layer_norm(summed.reshape(-1, channels), picture_token_layer_scaling).astype(
        jnp.bfloat16
    )
    lat_norm = layer_norm(summary_probes.astype(jnp.float32), summary_probe_layer_scaling).astype(
        jnp.bfloat16
    )
    tok_count = tok_norm.shape[0]
    shard_rows = asking_projection_tensor.shape[0]
    first_row = lax.axis_index("wide") * shard_rows
    lat_slice = lax.dynamic_slice_in_dim(lat_norm, first_row, shard_rows, 1)
    probe_asking_vectors = lax.psum(
        jnp.dot(lat_slice, asking_projection_tensor, preferred_element_type=jnp.float32), "wide"
    )
    rescaled_similarity_logits = (
        probe_asking_vectors.reshape(lat_count, subspace_number_overall, subspace_breadth)
        * (sharpness_coefficient / math.sqrt(subspace_breadth))[None, :, None]
    )
    key_source = jnp.concatenate([tok_norm, lat_norm], axis=0)
    zero_rows = jnp.zeros((key_source.shape[0], channels), jnp.float32)

    def add_rows(running, weight_rows):
        return running + jnp.dot(key_source, weight_rows, preferred_element_type=jnp.float32)

    def scores_of(key_part):
        return jnp.einsum(
            "lhd,thd->hlt",
            rescaled_similarity_logits,
            key_part.reshape(-1, subspace_number_overall, subspace_breadth),
            precision=lax.Precision.HIGHEST,
        )

    running = (zero_rows, zero_rows)
    weight_rows = (
        lax.all_gather(lookup_projection_tensor, "wide", axis=0, tiled=True),
        lax.all_gather(content_projection_tensor, "wide", axis=0, tiled=True),
    )
    key_proj = add_rows(running[0], weight_rows[0])
    value_proj = add_rows(running[1], weight_rows[1])
    tok_terms = softmax_terms(
        scores_of(key_proj[:tok_count]),
        value_proj[:tok_count].reshape(-1, subspace_number_overall, subspace_breadth),
    )
    lat_terms = softmax_terms(
        scores_of(key_proj[tok_count:]),
        value_proj[tok_count:].reshape(-1, subspace_number_overall, subspace_breadth),
    )
    merged = merge_all(*tok_terms)
    joint_max, joint_sum, joint_weighted = combine(merged, lat_terms)
    attention = (
        (joint_weighted / joint_sum[..., None]).transpose(1, 0, 2).reshape(lat_count, channels)
    )
    attention_low = attention.astype(jnp.bfloat16)
    out_cols = jnp.dot(attention_low, final_projection_tensor, preferred_element_type=jnp.float32)
    attended = lax.all_gather(out_cols, "wide", axis=1, tiled=True)
    new_latents = (summary_probes.astype(jnp.float32) + attended).astype(jnp.bfloat16)
    return (attended, new_latents)


def solution(mesh):
    placed = (
        P(("groups", "wide"), None, None, None),
        P(),
        P(),
        P(),
        P(),
        P("wide", None),
        P("wide", None),
        P("wide", None),
        P(None, "wide"),
        P(),
    )
    return jax.shard_map(
        per_device,
        mesh=mesh,
        in_specs=placed,
        out_specs=(P("groups", None), P("groups", None)),
        check_vma=False,
    )
```

profile of v0, /device:TPU:0, one launch (start us, length us, event | category | flops | bytes accessed | tf_op | source)
XLA Modules:
  0.0 424.6 jit_solution(6361989302038620171)
XLA Ops:
  7.2 0.7 all-gather.4.cloned.1.call-update
  8.0 0.7 all-gather.6.cloned.1.call-update
  8.7 1.1 convert_reduce_fusion
  9.8 1.2 fusion.34
  11.0 1.1 fusion.36
  12.5 1.0 copy.42
  13.5 6.2 %copy.43 = bf16[3,3,128,1536]{2,3,1,0:T(8,128)(2,1)} copy(bf16[3,3,128,1536]{3,2,1,0:T(8,128)(2,1)} %param.11) | data formatting | bytes 7077888 | tf_op args[1]
  19.7 9.5 %fusion.55 = (f32[8,10,10]{0,2,1:T(8,128)S(1)}, f32[8,10,10,1536]{3,0,2,1:T(8,128)}) fusion(bf16[3,3,128,12,128]{2,4,3,1,0:T(8,128)(2,1)} %bitcast.34, bf16[8,10,10,1536]{3,0,2,1:T(8,128)(2,1)S(1)} %copy-done.9), kind=kOutput, calls=%fused_computation.74 | convolution fusion | flops 2483453184 | bytes 10914944 | tf_op jit(solution)/shard_map/conv_general_dilated | solution.py:62
  29.5 8.7 %copy.44 = f32[8,10,10,1536]{3,2,1,0:T(8,128)} copy(f32[8,10,10,1536]{3,0,2,1:T(8,128)} %get-tuple-element.8) | data formatting | bytes 9830400 | tf_op jit(solution)/shard_map/add | solution.py:71
  38.2 0.6 multiply_reduce_fusion
  39.1 6.6 %reshape.83 = f32[800,1536]{1,0:T(8,128)} reshape(f32[8,10,10,1536]{3,2,1,0:T(8,128)} %copy.44) | data formatting | bytes 9830400 | tf_op jit(solution)/shard_map/reshape | solution.py:72
  45.9 3.1 multiply_convert_fusion
  49.0 17.4 %all-gather.4.cloned.1.call-done = bf16[1536,1536]{1,0:T(8,128)(2,1)} async-done(((bf16[96,1536]{1,0:T(8,128)(2,1)}), bf16[1536,1536]{1,0:T(8,128)(2,1)}) %all-gather.4.cloned.1.call-update) | async-done | bytes 4718608 | tf_op jit(solution)/shard_map/all_gather | solution.py:105
  66.4 8.6 %fusion.19 = f32[864,1536]{1,0:T(8,128)} fusion(bf16[1536,1536]{1,0:T(8,128)(2,1)} %all-gather.4.cloned.1.call-done, bf16[64,1536]{1,0:T(8,128)(2,1)S(1)} %fusion.36, bf16[800,1536]{1,0:T(8,128)(2,1)S(1)} %multiply_convert_fusion), kind=kOutput, calls=%fused_computation.25 | convolution fusion | flops 4082171904 | bytes 12681216 | tf_op jit(solution)/shard_map/dot_general | solution.py:93
  75.0 45.7 %all-gather.6.cloned.1.call-done = bf16[1536,1536]{1,0:T(8,128)(2,1)} async-done(((bf16[96,1536]{1,0:T(8,128)(2,1)}), bf16[1536,1536]{1,0:T(8,128)(2,1)}) %all-gather.6.cloned.1.call-update) | async-done | bytes 4718608 | tf_op jit(solution)/shard_map/all_gather | solution.py:106
  120.7 6.5 %fusion.18 = f32[864,1536]{1,0:T(8,128)S(1)} fusion(bf16[1536,1536]{1,0:T(8,128)(2,1)} %all-gather.6.cloned.1.call-done, bf16[64,1536]{1,0:T(8,128)(2,1)S(1)} %fusion.36, bf16[800,1536]{1,0:T(8,128)(2,1)S(1)} %multiply_convert_fusion), kind=kOutput, calls=%fused_computation.24 | convolution fusion | flops 4082171904 | bytes 12681216 | tf_op jit(solution)/shard_map/dot_general | solution.py:93
  127.2 2.8 slice.16
  130.0 2.5 slice.17
  132.5 6.0 %copy.50 = f32[800,1536]{0,1:T(8,128)} copy(f32[800,1536]{1,0:T(8,128)} %slice.16) | data formatting | bytes 9830400 | tf_op jit(solution)/shard_map/slice | solution.py:111
  138.5 74.2 %all-reduce.3.cloned.1.call-done = f32[64,16,96]{2,0,1:T(8,128)} async-done(((f32[64,16,96]{2,0,1:T(8,128)}), f32[64,16,96]{2,0,1:T(8,128)}) %all-reduce.3.cloned.1.call-update) | async-done | bytes 393232 | tf_op jit(solution)/shard_map/psum | solution.py:82
  212.7 8.3 %fusion.56 = (f32[16,64]{1,0:T(8,128)S(1)}, f32[16,64,800]{2,1,0:T(8,128)}) fusion(f32[800,16,96]{0,2,1:T(8,128)} %bitcast.30, f32[64,16,96]{2,0,1:T(8,128)} %all-reduce.3.cloned.1.call-done, f32[16]{0:T(128)S(1)} %broadcast_multiply_fusion.1), kind=kOutput, calls=%fused_computation.75 | convolution fusion | flops 944634880 | bytes 8589376 | tf_op jit(solution)/shard_map/lhd,thd->hlt/dot_general | solution.py:96
  221.0 32.4 %pmax.7 = f32[16,64]{1,0:T(8,128)S(1)} all-reduce(f32[16,64]{1,0:T(8,128)S(1)} %get-tuple-element.9), channel_id=1, replica_groups=mesh['groups'=2,'wide'=16] {'wide'}, use_global_device_ids=true, to_apply=%region_6.0 | all-reduce | flops 1024 | bytes 8192 | tf_op jit(solution)/shard_map/pmax | solution.py:31
  253.5 2.9 fusion.6
  256.4 30.0 %psum.23 = f32[16,64]{1,0:T(8,128)S(1)} all-reduce(f32[16,64]{1,0:T(8,128)S(1)} %get-tuple-element.5), channel_id=1, replica_groups=mesh['groups'=2,'wide'=16] {'wide'}, use_global_device_ids=true, to_apply=%region_10.0 | all-reduce | flops 1024 | bytes 8192 | tf_op jit(solution)/shard_map/psum | solution.py:33
  286.6 6.0 %copy.51 = f32[800,1536]{0,1:T(8,128)} copy(f32[800,1536]{1,0:T(8,128)} %slice.17) | data formatting | bytes 9830400 | tf_op jit(solution)/shard_map/slice | solution.py:112
  292.6 11.3 %fusion.20 = f32[16,64,96]{2,1,0:T(8,128)} fusion(f32[800,16,96]{0,2,1:T(8,128)} %bitcast.31, f32[16,64,800]{2,1,0:T(8,128)} %get-tuple-element.10, f32[16,64]{1,0:T(8,128)S(1)} %get-tuple-element.9, f32[16,64]{1,0:T(8,128)S(1)} %get-tuple-element.6), kind=kOutput, calls=%fused_computation.26 | convolution fusion | flops 944635904 | bytes 8593408 | tf_op jit(solution)/shard_map/hlt,thd->hld/dot_general | solution.py:41
  304.1 1.1 fusion.57
  305.4 85.9 %all-reduce.5.cloned.1.call-done = f32[16,64,96]{2,1,0:T(8,128)} async-done(((f32[16,64,96]{2,1,0:T(8,128)}), f32[16,64,96]{2,1,0:T(8,128)}) %all-reduce.5.cloned.1.call-update) | async-done | bytes 393232 | tf_op jit(solution)/shard_map/psum | solution.py:33
  391.3 2.5 fusion.24
  394.4 22.2 %all-gather = f32[16,96,64]{1,2,0:T(8,128)S(1)} all-gather(f32[1,96,64]{1,2,0:T(8,128)S(1)} %convolution_bitcast_fusion), channel_id=1, replica_groups=mesh['groups'=2,'wide'=16] {'wide'}, dimensions={0}, use_global_device_ids=true | all-gather | bytes 417792 | tf_op jit(solution)/shard_map/all_gather | solution.py:125
  416.7 0.3 copy.56
  417.2 0.8 fusion.37
  (60 shorter events, 2.8 us)
Async XLA Ops:
  7.2 4.9 %copy-start = (bf16[96,1536]{1,0:T(8,128)(2,1)S(1)}, bf16[96,1536]{1,0:T(8,128)(2,1)}, u32[]{:S(2)}) copy-start(bf16[96,1536]{1,0:T(8,128)(2,1)} %param.15) | copy-start | bytes 884740
  7.2 59.2 %all-gather.4.cloned.1.call-start = ((), (), s32[]{:S(2)}) async-start(), calls=%async_computation.1 | async-start | bytes 5013504 | tf_op jit(solution)/shard_map/all_gather | solution.py:105
  7.9 112.8 %all-gather.6.cloned.1.call-start = ((), (), s32[]{:S(2)}) async-start(), calls=%async_computation.2 | async-start | bytes 5013504 | tf_op jit(solution)/shard_map/all_gather | solution.py:106
  8.7 204.1 %all-reduce.3.cloned.1.call-start = ((), (), s32[]{:S(2)}) async-start(), calls=%async_computation | async-start | bytes 1048576 | tf_op jit(solution)/shard_map/psum | solution.py:82
  13.5 6.3 %copy-start.9 = (bf16[8,10,10,1536]{3,0,2,1:T(8,128)(2,1)S(1)}, bf16[8,10,10,1536]{3,0,2,1:T(8,128)(2,1)}, u32[]{:S(2)}) copy-start(bf16[8,10,10,1536]{3,0,2,1:T(8,128)(2,1)} %param.10) | copy-start | bytes 7372804
  13.5 377.8 %all-reduce.5.cloned.1.call-start = ((), (), s32[]{:S(2)}) async-start(), calls=%async_computation.3 | async-start | bytes 1048576 | tf_op jit(solution)/shard_map/psum | solution.py:33
  29.3 8.8 %slice-start = ((s8[4915200]{0:T(1024)(128)(4,1)}), s8[720896]{0:T(1024)(128)(4,1)S(1)}, s32[]{:S(2)}) async-start(s8[4915200]{0:T(1024)(128)(4,1)} %bitcast.32), calls=%async_computation.4 | async-start | bytes 1441792
  29.5 8.7 %slice-start.1 = ((s8[4915200]{0:T(1024)(128)(4,1)}), s8[4194304]{0:T(1024)(128)(4,1)S(1)}, s32[]{:S(2)}) async-start(s8[4915200]{0:T(1024)(128)(4,1)} %bitcast.32), calls=%async_computation.5 | async-start | bytes 8388608
  39.1 6.8 %copy-start.10 = (f32[16]{0:T(128)S(1)}, f32[16]{0:T(128)}, u32[]{:S(2)}) copy-start(f32[16]{0:T(128)} %param.19) | copy-start | bytes 196
  39.1 6.8 %copy-start.8 = (f32[1536]{0:T(1024)S(1)}, f32[1536]{0:T(1024)}, u32[]{:S(2)}) copy-start(f32[1536]{0:T(1024)} %param.12) | copy-start | bytes 18436
  120.7 6.5 %copy-start.2 = (f32[864,1536]{1,0:T(8,128)S(1)}, f32[864,1536]{1,0:T(8,128)}, u32[]{:S(2)}) copy-start(f32[864,1536]{1,0:T(8,128)} %fusion.19) | copy-start | bytes 15925252
  127.2 5.4 %copy-start.3 = (f32[864,1536]{1,0:T(8,128)}, f32[864,1536]{1,0:T(8,128)S(1)}, u32[]{:S(2)}) copy-start(f32[864,1536]{1,0:T(8,128)S(1)} %fusion.18) | copy-start | bytes 15925252
  212.7 73.7 %slice-start.2 = ((f32[864,1536]{1,0:T(8,128)}), f32[64,1536]{1,0:T(8,128)S(1)}, s32[]{:S(2)}) async-start(f32[864,1536]{1,0:T(8,128)} %fusion.19), calls=%async_computation.6 | async-start | bytes 786432 | tf_op jit(solution)/shard_map/slice | solution.py:115
  292.5 11.3 %slice-start.3 = ((f32[864,1536]{1,0:T(8,128)}), f32[64,1536]{1,0:T(8,128)S(1)}, s32[]{:S(2)}) async-start(f32[864,1536]{1,0:T(8,128)} %copy-done.3), calls=%async_computation.7 | async-start | bytes 786432 | tf_op jit(solution)/shard_map/slice | solution.py:116
  292.6 11.5 %copy-start.5 = (f32[64,16,96]{2,0,1:T(8,128)S(1)}, f32[64,16,96]{2,0,1:T(8,128)}, u32[]{:S(2)}) copy-start(f32[64,16,96]{2,0,1:T(8,128)} %all-reduce.3.cloned.1.call-done) | copy-start | bytes 1179652
  303.8 90.4 %copy-start.7 = (bf16[1536,96]{0,1:T(8,128)(2,1)S(1)}, bf16[1536,96]{0,1:T(8,128)(2,1)}, u32[]{:S(2)}) copy-start(bf16[1536,96]{0,1:T(8,128)(2,1)} %param.18) | copy-start | bytes 884740
  303.9 113.4 %copy-start.4 = (bf16[64,1536]{1,0:T(8,128)(2,1)S(1)}, bf16[64,1536]{1,0:T(8,128)(2,1)}, u32[]{:S(2)}) copy-start(bf16[64,1536]{1,0:T(8,128)(2,1)} %param.13) | copy-start | bytes 589828
  303.9 114.2 %copy-start.1 = (bf16[96,1536]{1,0:T(8,128)(2,1)S(1)}, bf16[96,1536]{1,0:T(8,128)(2,1)}, u32[]{:S(2)}) copy-start(bf16[96,1536]{1,0:T(8,128)(2,1)} %param.15) | copy-start | bytes 884740
  417.2 0.8 copy-start.6
Sparse Core Ops, SparseCore 0:
  10.3 56.0 all-gather.3
  68.7 51.9 all-gather.5
  124.1 88.5 all-reduce.2
  304.0 87.2 all-reduce.4
where the time goes:
time: 425 us
  waiting for transfers between devices  225 us (53%)
  blocking collectives  84.7 us (20%)
  matrix products  48.2 us (11%)
  local copies, waits for them, and re-layouts  42 us (10%)
  between operations  14.1 us (3%)
  other arithmetic  10.9 us (3%)
    psum x1, waiting for transfers between devices, merge_all(): lax.psum((row_sum * factor, weighted * factor[..., None]), 'wide')  85.9 us
    psum x1, waiting for transfers between devices, per_device(): lax.psum(jnp.dot(lat_slice, asking_projection_tensor, preferred_element_t...  74.2 us
    all_gather x1, waiting for transfers between devices, per_device(): lax.all_gather(content_projection_tensor, 'wide', axis=0, tiled=True)  45.7 us
    pmax x1, blocking collectives, merge_all(): joint_max = lax.pmax(row_max, 'wide')  32.4 us
    psum x1, blocking collectives, merge_all(): lax.psum((row_sum * factor, weighted * factor[..., None]), 'wide')  30 us
    all_gather x1, blocking collectives, per_device(): attended = lax.all_gather(out_cols, 'wide', axis=1, tiled=True)  22.2 us
    all_gather x1, waiting for transfers between devices, per_device(): lax.all_gather(lookup_projection_tensor, 'wide', axis=0, tiled=True)  17.4 us
    dot_general x2, matrix products, add_rows(): jnp.dot(key_source, weight_rows, preferred_element_type=jnp.float32)  15 us
  transfers between devices with their start and end apart: 4, of which 4 were waited for; matrix products, arithmetic and copies ran while one was open for 16% of the time, Pallas kernels for 0%

commit v1 on v0

--- a/solution.py
+++ b/solution.py
@@ -6,6 +6,19 @@
 
 RESIDUAL_SCALE = 0.2
 EPSILON = 1e-06
+
+
+def collect(x, axis, dim):
+    ways = lax.axis_size(axis)
+    up = [(d, (d + 1) % ways) for d in range(ways)]
+    down = [(d, (d - 1) % ways) for d in range(ways)]
+    earlier, later = ([x], [x])
+    for _ in range(ways // 2):
+        earlier.append(lax.ppermute(earlier[-1], axis, up))
+    for _ in range((ways - 1) // 2):
+        later.append(lax.ppermute(later[-1], axis, down))
+    line = jnp.concatenate([*earlier[::-1], *later[1:]], axis=dim)
+    return jnp.roll(line, (lax.axis_index(axis) - ways // 2) * x.shape[dim], axis=dim)
 
 
 def layer_norm(values, gain):
@@ -102,7 +115,7 @@
 
     running = (zero_rows, zero_rows)
     weight_rows = (
-        lax.all_gather(lookup_projection_tensor, "wide", axis=0, tiled=True),
+        collect(lookup_projection_tensor, "wide", 0),
         lax.all_gather(content_projection_tensor, "wide", axis=0, tiled=True),
     )
     key_proj = add_rows(running[0], weight_rows[0])

time: 425 us -> 370 us (0.87)
  waiting for transfers between devices: 225 us -> 113 us
  starting transfers between devices: 0.16 us -> 32.4 us
  local copies, waits for them, and re-layouts: 42 us -> 62.4 us
    psum x1, waiting for transfers between devices: 74.2 us -> 5.61 us  [per_device(): lax.psum(jnp.dot(lat_slice, asking_projection_tensor, preferred_element_t...]
    all_gather x1, waiting for transfers between devices: 45.7 us -> 0.02 us  [per_device(): lax.all_gather(content_projection_tensor, 'wide', axis=0, tiled=True)]
    ppermute x0 -> x15, starting transfers between devices: none -> 32.3 us  [the longest x7 31.7 us: collect(): later.append(lax.ppermute(later[-1], axis, down))]
    ppermute x0 -> x15, waiting for transfers between devices: none -> 19.6 us  [the longest x8 19.1 us: collect(): earlier.append(lax.ppermute(earlier[-1], axis, up))]
    unnamed x28 -> x87, local copies, waits for them, and re-layouts: 6.53 us -> 25.6 us
    all_gather x1 -> x0, waiting for transfers between devices: 17.4 us -> none  [per_device(): lax.all_gather(lookup_projection_tensor, 'wide', axis=0, tiled=True)]
    dot_general x2, matrix products: 15 us -> 10.5 us  [add_rows(): jnp.dot(key_source, weight_rows, preferred_element_type=jnp.float32)]
  transfers between devices with their start and end apart: 4 -> 18, of which waited for: 4 -> 8; matrix products, arithmetic and copies ran while one was open for 16% -> 24% of each run, Pallas kernels for 0% -> 0%
where the time goes in v1:
time: 370 us; the launch traced here: 369 us
  waiting for transfers between devices  113 us (31%)
  blocking collectives  85.9 us (23%)
  local copies, waits for them, and re-layouts  62.4 us (17%)
  matrix products  45.9 us (12%)
  starting transfers between devices  32.4 us (9%)
  between operations  14.5 us (4%)
  other arithmetic  14.4 us (4%)
    psum x1, waiting for transfers between devices, merge_all(): lax.psum((row_sum * factor, weighted * factor[..., None]), 'wide')  87.2 us
    pmax x1, blocking collectives, merge_all(): joint_max = lax.pmax(row_max, 'wide')  33.2 us
    ppermute x7, starting transfers between devices, collect(): later.append(lax.ppermute(later[-1], axis, down))  31.7 us
    psum x1, blocking collectives, merge_all(): lax.psum((row_sum * factor, weighted * factor[..., None]), 'wide')  30.4 us
    unnamed x87, local copies, waits for them, and re-layouts  25.6 us
    all_gather x1, blocking collectives, per_device(): attended = lax.all_gather(out_cols, 'wide', axis=1, tiled=True)  22.2 us
    ppermute x8, waiting for transfers between devices, collect(): earlier.append(lax.ppermute(earlier[-1], axis, up))  19.1 us
    dot_general x2, matrix products, softmax_terms(): jnp.einsum('hlt,thd->hld', weights, carried, precision=lax.Precision.HIGH...  13.7 us
  transfers between devices with their start and end apart: 18, of which 8 were waited for; matrix products, arithmetic and copies ran while one was open for 24% of the time, Pallas kernels for 0%

profile of v1, /device:TPU:0, one launch (start us, length us, event | category | flops | bytes accessed | tf_op | source)
XLA Modules:
  0.0 368.7 jit_solution(5779345344132242396)
XLA Ops:
  7.7 5.1 %collective-permute-start.8 = (bf16[96,1536]{1,0:T(8,128)(2,1)}, bf16[96,1536]{1,0:T(8,128)(2,1)S(1)}, u32[]{:S(2)}, u32[]{:S(2)}) collective-permute-start(bf16[96,1536]{1,0:T(8,128)(2,1)} %param.16), channel_id=1, source_target_pairs={{0,15},{1,0},{2,1},{3,2},{4,3},{5,4},{6,5},{7,6},{8,7},{9,8},{10,9... | collective-permute-start | bytes 884744 | tf_op jit(solution)/shard_map/ppermute | solution.py:19
  12.8 4.7 %collective-permute-done = bf16[96,1536]{1,0:T(8,128)(2,1)S(1)} collective-permute-done((bf16[96,1536]{1,0:T(8,128)(2,1)}, bf16[96,1536]{1,0:T(8,128)(2,1)S(1)}, u32[]{:S(2)}, u32[]{:S(2)}) %collective-permute-start) | collective-permute-done | bytes 294944 | tf_op jit(solution)/shard_map/ppermute | solution.py:17
  18.6 7.7 %collective-permute-done.1 = bf16[96,1536]{1,0:T(8,128)(2,1)S(1)} collective-permute-done((bf16[96,1536]{1,0:T(8,128)(2,1)S(1)}, bf16[96,1536]{1,0:T(8,128)(2,1)S(1)}, u32[]{:S(2)}, u32[]{:S(2)}) %collective-permute-start.1) | collective-permute-done | bytes 294944 | tf_op jit(solution)/shard_map/ppermute | solution.py:17
  27.6 4.4 %collective-permute-start.9 = (bf16[96,1536]{1,0:T(8,128)(2,1)S(1)}, bf16[96,1536]{1,0:T(8,128)(2,1)S(1)}, u32[]{:S(2)}, u32[]{:S(2)}) collective-permute-start(bf16[96,1536]{1,0:T(8,128)(2,1)S(1)} %collective-permute-done.8), channel_id=1, source_target_pairs={{0,15},{1,0},{2,1},{3,2},{4,3},{5,4},{6,5},{7,6},{8,7},{9,8},{10,9... | collective-permute-start | bytes 884744 | tf_op jit(solution)/shard_map/ppermute | solution.py:19
  32.0 3.3 collective-permute-done.2
  36.5 4.5 %collective-permute-start.10 = (bf16[96,1536]{1,0:T(8,128)(2,1)S(1)}, bf16[96,1536]{1,0:T(8,128)(2,1)S(1)}, u32[]{:S(2)}, u32[]{:S(2)}) collective-permute-start(bf16[96,1536]{1,0:T(8,128)(2,1)S(1)} %collective-permute-done.9), channel_id=1, source_target_pairs={{0,15},{1,0},{2,1},{3,2},{4,3},{5,4},{6,5},{7,6},{8,7},{9,8},{10,9... | collective-permute-start | bytes 884744 | tf_op jit(solution)/shard_map/ppermute | solution.py:19
  40.9 3.3 collective-permute-done.3
  46.5 6.0 %copy.43 = bf16[3,3,128,1536]{2,3,1,0:T(8,128)(2,1)} copy(bf16[3,3,128,1536]{3,2,1,0:T(8,128)(2,1)} %param.11) | data formatting | bytes 7077888 | tf_op args[1]
  52.5 4.4 %collective-permute-start.11 = (bf16[96,1536]{1,0:T(8,128)(2,1)S(1)}, bf16[96,1536]{1,0:T(8,128)(2,1)S(1)}, u32[]{:S(2)}, u32[]{:S(2)}) collective-permute-start(bf16[96,1536]{1,0:T(8,128)(2,1)S(1)} %collective-permute-done.10), channel_id=1, source_target_pairs={{0,15},{1,0},{2,1},{3,2},{4,3},{5,4},{6,5},{7,6},{8,7},{9,8},{10,9... | collective-permute-start | bytes 884744 | tf_op jit(solution)/shard_map/ppermute | solution.py:19
  56.9 10.8 %fusion.57 = (f32[8,10,10]{0,2,1:T(8,128)S(1)}, f32[8,10,10,1536]{3,0,2,1:T(8,128)}) fusion(bf16[3,3,128,12,128]{2,4,3,1,0:T(8,128)(2,1)} %bitcast.31, bf16[8,10,10,1536]{3,0,2,1:T(8,128)(2,1)} %param.10), kind=kOutput, calls=%fused_computation.108 | convolution fusion | flops 2483453184 | bytes 10914944 | tf_op jit(solution)/shard_map/conv_general_dilated | solution.py:75
  68.0 4.4 %collective-permute-start.12 = (bf16[96,1536]{1,0:T(8,128)(2,1)S(1)}, bf16[96,1536]{1,0:T(8,128)(2,1)}, u32[]{:S(2)}, u32[]{:S(2)}) collective-permute-start(bf16[96,1536]{1,0:T(8,128)(2,1)S(1)} %collective-permute-done.11), channel_id=1, source_target_pairs={{0,15},{1,0},{2,1},{3,2},{4,3},{5,4},{6,5},{7,6},{8,7},{9,8},{10,9... | collective-permute-start | bytes 884744 | tf_op jit(solution)/shard_map/ppermute | solution.py:19
  72.5 3.2 multiply_reduce_fusion
  75.6 8.5 %copy.44 = f32[8,10,10,1536]{3,2,1,0:T(8,128)} copy(f32[8,10,10,1536]{3,0,2,1:T(8,128)} %get-tuple-element.8) | data formatting | bytes 9830400 | tf_op jit(solution)/shard_map/add | solution.py:84
  84.4 7.3 %reshape.83 = f32[800,1536]{1,0:T(8,128)} reshape(f32[8,10,10,1536]{3,2,1,0:T(8,128)} %copy.44) | data formatting | bytes 9830400 | tf_op jit(solution)/shard_map/reshape | solution.py:85
  91.9 4.3 %collective-permute-start.13 = (bf16[96,1536]{1,0:T(8,128)(2,1)}, bf16[96,1536]{1,0:T(8,128)(2,1)}, u32[]{:S(2)}, u32[]{:S(2)}) collective-permute-start(bf16[96,1536]{1,0:T(8,128)(2,1)} %collective-permute-done.12), channel_id=1, source_target_pairs={{0,15},{1,0},{2,1},{3,2},{4,3},{5,4},{6,5},{7,6},{8,7},{9,8},{10,9... | collective-permute-start | bytes 884744 | tf_op jit(solution)/shard_map/ppermute | solution.py:19
  96.2 3.1 multiply_convert_fusion
  100.8 4.6 %collective-permute-start.14 = (bf16[96,1536]{1,0:T(8,128)(2,1)}, bf16[96,1536]{1,0:T(8,128)(2,1)S(1)}, u32[]{:S(2)}, u32[]{:S(2)}) collective-permute-start(bf16[96,1536]{1,0:T(8,128)(2,1)} %collective-permute-done.13), channel_id=1, source_target_pairs={{0,15},{1,0},{2,1},{3,2},{4,3},{5,4},{6,5},{7,6},{8,7},{9,8},{10,9... | collective-permute-start | bytes 884744 | tf_op jit(solution)/shard_map/ppermute | solution.py:19
  121.9 4.3 %fusion.6 = f32[864,1536]{1,0:T(8,128)S(1)} fusion(bf16[3072,1536]{1,0:T(8,128)(2,1)S(1)} %constant_dynamic-update-slice_fusion, s32[]{:T(128)S(6)} %select_n.18, bf16[64,1536]{1,0:T(8,128)(2,1)S(1)} %fusion.37, bf16[800,1536]{1,0:T(8,128)(2,1)S(1)} %multiply_convert_fusion), kind=kOutput, calls=%fused_computation.13 | convolution fusion | flops 4082171904 | bytes 12681220 | tf_op jit(solution)/shard_map/dot_general | solution.py:106
  126.3 2.6 slice.16
  129.8 6.0 %copy.50 = f32[800,1536]{0,1:T(8,128)} copy(f32[800,1536]{1,0:T(8,128)} %slice.16) | data formatting | bytes 9830400 | tf_op jit(solution)/shard_map/slice | solution.py:124
  135.8 5.6 %all-reduce.3.cloned.1.call-done = f32[64,16,96]{2,0,1:T(8,128)} async-done(((f32[64,16,96]{2,0,1:T(8,128)}), f32[64,16,96]{2,0,1:T(8,128)}) %all-reduce.3.cloned.1.call-update) | async-done | bytes 393232 | tf_op jit(solution)/shard_map/psum | solution.py:95
  141.5 8.3 %fusion.58 = (f32[16,64]{1,0:T(8,128)S(1)}, f32[16,64,800]{2,1,0:T(8,128)}) fusion(f32[800,16,96]{0,2,1:T(8,128)} %bitcast.29, f32[64,16,96]{2,0,1:T(8,128)} %all-reduce.3.cloned.1.call-done, f32[16]{0:T(128)S(1)} %broadcast_multiply_fusion.1), kind=kOutput, calls=%fused_computation.109 | convolution fusion | flops 944634880 | bytes 8589376 | tf_op jit(solution)/shard_map/lhd,thd->hlt/dot_general | solution.py:109
  149.8 33.2 %pmax.7 = f32[16,64]{1,0:T(8,128)S(1)} all-reduce(f32[16,64]{1,0:T(8,128)S(1)} %get-tuple-element.9), channel_id=1, replica_groups=mesh['groups'=2,'wide'=16] {'wide'}, use_global_device_ids=true, to_apply=%region_6.7 | all-reduce | flops 1024 | bytes 8192 | tf_op jit(solution)/shard_map/pmax | solution.py:44
  183.0 2.9 fusion.8
  185.9 30.4 %psum.23 = f32[16,64]{1,0:T(8,128)S(1)} all-reduce(f32[16,64]{1,0:T(8,128)S(1)} %get-tuple-element.5), channel_id=1, replica_groups=mesh['groups'=2,'wide'=16] {'wide'}, use_global_device_ids=true, to_apply=%region_10.11 | all-reduce | flops 1024 | bytes 8192 | tf_op jit(solution)/shard_map/psum | solution.py:46
  219.5 6.1 %fusion.20 = f32[864,1536]{1,0:T(8,128)S(1)} fusion(bf16[1536,1536]{1,0:T(8,128)(2,1)} %all-gather.3.cloned.1.call-done, bf16[64,1536]{1,0:T(8,128)(2,1)S(1)} %fusion.37, bf16[800,1536]{1,0:T(8,128)(2,1)S(1)} %multiply_convert_fusion), kind=kOutput, calls=%fused_computation.26 | convolution fusion | flops 4082171904 | bytes 12681216 | tf_op jit(solution)/shard_map/dot_general | solution.py:106
  228.0 2.6 slice.17
  230.6 6.1 %copy.51 = f32[800,1536]{0,1:T(8,128)} copy(f32[800,1536]{1,0:T(8,128)} %slice.17) | data formatting | bytes 9830400 | tf_op jit(solution)/shard_map/slice | solution.py:125
  236.7 11.3 %fusion.21 = f32[16,64,96]{2,1,0:T(8,128)} fusion(f32[800,16,96]{0,2,1:T(8,128)} %bitcast.30, f32[16,64,800]{2,1,0:T(8,128)} %get-tuple-element.10, f32[16,64]{1,0:T(8,128)S(1)} %get-tuple-element.9, f32[16,64]{1,0:T(8,128)S(1)} %get-tuple-element.6), kind=kOutput, calls=%fused_computation.27 | convolution fusion | flops 944635904 | bytes 8593408 | tf_op jit(solution)/shard_map/hlt,thd->hld/dot_general | solution.py:54
  248.2 87.2 %all-reduce.5.cloned.1.call-done = f32[16,64,96]{2,1,0:T(8,128)} async-done(((f32[16,64,96]{2,1,0:T(8,128)}), f32[16,64,96]{2,1,0:T(8,128)}) %all-reduce.5.cloned.1.call-update) | async-done | bytes 393232 | tf_op jit(solution)/shard_map/psum | solution.py:46
  335.4 2.5 fusion.25
  338.6 22.2 %all-gather = f32[16,96,64]{1,2,0:T(8,128)S(1)} all-gather(f32[1,96,64]{1,2,0:T(8,128)S(1)} %convolution_bitcast_fusion), channel_id=1, replica_groups=mesh['groups'=2,'wide'=16] {'wide'}, dimensions={0}, use_global_device_ids=true | all-gather | bytes 417792 | tf_op jit(solution)/shard_map/all_gather | solution.py:138
  (145 shorter events, 33.5 us)
Async XLA Ops:
  7.2 37.1 %copy-start = (bf16[96,1536]{1,0:T(8,128)(2,1)S(1)}, bf16[96,1536]{1,0:T(8,128)(2,1)}, u32[]{:S(2)}) copy-start(bf16[96,1536]{1,0:T(8,128)(2,1)} %param.15) | copy-start | bytes 884740
  7.2 134.3 %all-reduce.3.cloned.1.call-start = ((), (), s32[]{:S(2)}) async-start(), calls=%async_computation | async-start | bytes 1048576 | tf_op jit(solution)/shard_map/psum | solution.py:95
  7.2 10.2 %collective-permute-start = (bf16[96,1536]{1,0:T(8,128)(2,1)}, bf16[96,1536]{1,0:T(8,128)(2,1)S(1)}, u32[]{:S(2)}, u32[]{:S(2)}) collective-permute-start(bf16[96,1536]{1,0:T(8,128)(2,1)} %param.16), channel_id=1, source_target_pairs={{0,1},{1,2},{2,3},{3,4},{4,5},{5,6},{6,7},{7,8},{8,9},{9,10},{10,1... | collective-permute-start | bytes 884744 | tf_op jit(solution)/shard_map/ppermute | solution.py:17
  7.7 19.8 %collective-permute-start.8 = (bf16[96,1536]{1,0:T(8,128)(2,1)}, bf16[96,1536]{1,0:T(8,128)(2,1)S(1)}, u32[]{:S(2)}, u32[]{:S(2)}) collective-permute-start(bf16[96,1536]{1,0:T(8,128)(2,1)} %param.16), channel_id=1, source_target_pairs={{0,15},{1,0},{2,1},{3,2},{4,3},{5,4},{6,5},{7,6},{8,7},{9,8},{10,9... | collective-permute-start | bytes 884744 | tf_op jit(solution)/shard_map/ppermute | solution.py:19
  17.5 8.8 %collective-permute-start.1 = (bf16[96,1536]{1,0:T(8,128)(2,1)S(1)}, bf16[96,1536]{1,0:T(8,128)(2,1)S(1)}, u32[]{:S(2)}, u32[]{:S(2)}) collective-permute-start(bf16[96,1536]{1,0:T(8,128)(2,1)S(1)} %collective-permute-done), channel_id=1, source_target_pairs={{0,1},{1,2},{2,3},{3,4},{4,5},{5,6},{6,7},{7,8},{8,9},{9,10},{10,1... | collective-permute-start | bytes 884744 | tf_op jit(solution)/shard_map/ppermute | solution.py:17
  26.3 9.0 %collective-permute-start.2 = (bf16[96,1536]{1,0:T(8,128)(2,1)S(1)}, bf16[96,1536]{1,0:T(8,128)(2,1)S(1)}, u32[]{:S(2)}, u32[]{:S(2)}) collective-permute-start(bf16[96,1536]{1,0:T(8,128)(2,1)S(1)} %collective-permute-done.1), channel_id=1, source_target_pairs={{0,1},{1,2},{2,3},{3,4},{4,5},{5,6},{6,7},{7,8},{8,9},{9,10},{10,1... | collective-permute-start | bytes 884744 | tf_op jit(solution)/shard_map/ppermute | solution.py:17
  27.6 8.9 %collective-permute-start.9 = (bf16[96,1536]{1,0:T(8,128)(2,1)S(1)}, bf16[96,1536]{1,0:T(8,128)(2,1)S(1)}, u32[]{:S(2)}, u32[]{:S(2)}) collective-permute-start(bf16[96,1536]{1,0:T(8,128)(2,1)S(1)} %collective-permute-done.8), channel_id=1, source_target_pairs={{0,15},{1,0},{2,1},{3,2},{4,3},{5,4},{6,5},{7,6},{8,7},{9,8},{10,9... | collective-permute-start | bytes 884744 | tf_op jit(solution)/shard_map/ppermute | solution.py:19
  35.3 32.5 %copy-start.13 = (bf16[96,1536]{1,0:T(8,128)(2,1)}, bf16[96,1536]{1,0:T(8,128)(2,1)S(1)}, u32[]{:S(2)}) copy-start(bf16[96,1536]{1,0:T(8,128)(2,1)S(1)} %collective-permute-done.2) | copy-start | bytes 884740
  35.3 9.0 %collective-permute-start.3 = (bf16[96,1536]{1,0:T(8,128)(2,1)S(1)}, bf16[96,1536]{1,0:T(8,128)(2,1)S(1)}, u32[]{:S(2)}, u32[]{:S(2)}) collective-permute-start(bf16[96,1536]{1,0:T(8,128)(2,1)S(1)} %collective-permute-done.2), channel_id=1, source_target_pairs={{0,1},{1,2},{2,3},{3,4},{4,5},{5,6},{6,7},{7,8},{8,9},{9,10},{10,1... | collective-permute-start | bytes 884744 | tf_op jit(solution)/shard_map/ppermute | solution.py:17
  36.4 31.3 %copy-start.11 = (bf16[96,1536]{1,0:T(8,128)(2,1)}, bf16[96,1536]{1,0:T(8,128)(2,1)S(1)}, u32[]{:S(2)}) copy-start(bf16[96,1536]{1,0:T(8,128)(2,1)S(1)} %collective-permute-done.9) | copy-start | bytes 884740
  36.5 16.0 %collective-permute-start.10 = (bf16[96,1536]{1,0:T(8,128)(2,1)S(1)}, bf16[96,1536]{1,0:T(8,128)(2,1)S(1)}, u32[]{:S(2)}, u32[]{:S(2)}) collective-permute-start(bf16[96,1536]{1,0:T(8,128)(2,1)S(1)} %collective-permute-done.9), channel_id=1, source_target_pairs={{0,15},{1,0},{2,1},{3,2},{4,3},{5,4},{6,5},{7,6},{8,7},{9,8},{10,9... | collective-permute-start | bytes 884744 | tf_op jit(solution)/shard_map/ppermute | solution.py:19
  44.2 23.5 %copy-start.17 = (bf16[96,1536]{1,0:T(8,128)(2,1)}, bf16[96,1536]{1,0:T(8,128)(2,1)S(1)}, u32[]{:S(2)}) copy-start(bf16[96,1536]{1,0:T(8,128)(2,1)S(1)} %collective-permute-done.3) | copy-start | bytes 884740
  44.2 12.7 %collective-permute-start.4 = (bf16[96,1536]{1,0:T(8,128)(2,1)S(1)}, bf16[96,1536]{1,0:T(8,128)(2,1)S(1)}, u32[]{:S(2)}, u32[]{:S(2)}) collective-permute-start(bf16[96,1536]{1,0:T(8,128)(2,1)S(1)} %collective-permute-done.3), channel_id=1, source_target_pairs={{0,1},{1,2},{2,3},{3,4},{4,5},{5,6},{6,7},{7,8},{8,9},{9,10},{10,1... | collective-permute-start | bytes 884744 | tf_op jit(solution)/shard_map/ppermute | solution.py:17
  45.7 173.8 %all-gather.3.cloned.1.call-start = ((), (), s32[]{:S(2)}) async-start(), calls=%async_computation.1 | async-start | bytes 5013504 | tf_op jit(solution)/shard_map/all_gather | solution.py:119
  46.4 289.0 %all-reduce.5.cloned.1.call-start = ((), (), s32[]{:S(2)}) async-start(), calls=%async_computation.2 | async-start | bytes 1048576 | tf_op jit(solution)/shard_map/psum | solution.py:46
  52.5 15.6 %collective-permute-start.11 = (bf16[96,1536]{1,0:T(8,128)(2,1)S(1)}, bf16[96,1536]{1,0:T(8,128)(2,1)S(1)}, u32[]{:S(2)}, u32[]{:S(2)}) collective-permute-start(bf16[96,1536]{1,0:T(8,128)(2,1)S(1)} %collective-permute-done.10), channel_id=1, source_target_pairs={{0,15},{1,0},{2,1},{3,2},{4,3},{5,4},{6,5},{7,6},{8,7},{9,8},{10,9... | collective-permute-start | bytes 884744 | tf_op jit(solution)/shard_map/ppermute | solution.py:19
  56.9 15.6 %collective-permute-start.5 = (bf16[96,1536]{1,0:T(8,128)(2,1)S(1)}, bf16[96,1536]{1,0:T(8,128)(2,1)S(1)}, u32[]{:S(2)}, u32[]{:S(2)}) collective-permute-start(bf16[96,1536]{1,0:T(8,128)(2,1)S(1)} %collective-permute-done.4), channel_id=1, source_target_pairs={{0,1},{1,2},{2,3},{3,4},{4,5},{5,6},{6,7},{7,8},{8,9},{9,10},{10,1... | collective-permute-start | bytes 884744 | tf_op jit(solution)/shard_map/ppermute | solution.py:17
  68.0 23.7 %copy-start.21 = (bf16[96,1536]{1,0:T(8,128)(2,1)}, bf16[96,1536]{1,0:T(8,128)(2,1)S(1)}, u32[]{:S(2)}) copy-start(bf16[96,1536]{1,0:T(8,128)(2,1)S(1)} %collective-permute-done.11) | copy-start | bytes 884740
  68.0 23.8 %collective-permute-start.12 = (bf16[96,1536]{1,0:T(8,128)(2,1)S(1)}, bf16[96,1536]{1,0:T(8,128)(2,1)}, u32[]{:S(2)}, u32[]{:S(2)}) collective-permute-start(bf16[96,1536]{1,0:T(8,128)(2,1)S(1)} %collective-permute-done.11), channel_id=1, source_target_pairs={{0,15},{1,0},{2,1},{3,2},{4,3},{5,4},{6,5},{7,6},{8,7},{9,8},{10,9... | collective-permute-start | bytes 884744 | tf_op jit(solution)/shard_map/ppermute | solution.py:19
  72.4 23.8 %collective-permute-start.6 = (bf16[96,1536]{1,0:T(8,128)(2,1)S(1)}, bf16[96,1536]{1,0:T(8,128)(2,1)}, u32[]{:S(2)}, u32[]{:S(2)}) collective-permute-start(bf16[96,1536]{1,0:T(8,128)(2,1)S(1)} %collective-permute-done.5), channel_id=1, source_target_pairs={{0,1},{1,2},{2,3},{3,4},{4,5},{5,6},{6,7},{7,8},{8,9},{9,10},{10,1... | collective-permute-start | bytes 884744 | tf_op jit(solution)/shard_map/ppermute | solution.py:17
  84.4 28.0 %copy-start.8 = (bf16[96,1536]{1,0:T(8,128)(2,1)S(1)}, bf16[96,1536]{1,0:T(8,128)(2,1)}, u32[]{:S(2)}) copy-start(bf16[96,1536]{1,0:T(8,128)(2,1)} %param.16) | copy-start | bytes 884740
  91.9 8.9 %collective-permute-start.13 = (bf16[96,1536]{1,0:T(8,128)(2,1)}, bf16[96,1536]{1,0:T(8,128)(2,1)}, u32[]{:S(2)}, u32[]{:S(2)}) collective-permute-start(bf16[96,1536]{1,0:T(8,128)(2,1)} %collective-permute-done.12), channel_id=1, source_target_pairs={{0,15},{1,0},{2,1},{3,2},{4,3},{5,4},{6,5},{7,6},{8,7},{9,8},{10,9... | collective-permute-start | bytes 884744 | tf_op jit(solution)/shard_map/ppermute | solution.py:19
  96.2 9.3 %collective-permute-start.7 = (bf16[96,1536]{1,0:T(8,128)(2,1)}, bf16[96,1536]{1,0:T(8,128)(2,1)}, u32[]{:S(2)}, u32[]{:S(2)}) collective-permute-start(bf16[96,1536]{1,0:T(8,128)(2,1)} %collective-permute-done.6), channel_id=1, source_target_pairs={{0,1},{1,2},{2,3},{3,4},{4,5},{5,6},{6,7},{7,8},{8,9},{9,10},{10,1... | collective-permute-start | bytes 884744 | tf_op jit(solution)/shard_map/ppermute | solution.py:17
  99.4 20.4 %copy-start.12 = (bf16[96,1536]{1,0:T(8,128)(2,1)S(1)}, bf16[96,1536]{1,0:T(8,128)(2,1)}, u32[]{:S(2)}) copy-start(bf16[96,1536]{1,0:T(8,128)(2,1)} %copy-done.11) | copy-start | bytes 884740
  99.4 20.4 %copy-start.16 = (bf16[96,1536]{1,0:T(8,128)(2,1)S(1)}, bf16[96,1536]{1,0:T(8,128)(2,1)}, u32[]{:S(2)}) copy-start(bf16[96,1536]{1,0:T(8,128)(2,1)} %copy-done.15) | copy-start | bytes 884740
  99.4 20.5 %copy-start.22 = (bf16[96,1536]{1,0:T(8,128)(2,1)S(1)}, bf16[96,1536]{1,0:T(8,128)(2,1)}, u32[]{:S(2)}) copy-start(bf16[96,1536]{1,0:T(8,128)(2,1)} %copy-done.21) | copy-start | bytes 884740
  100.8 16.7 %collective-permute-start.14 = (bf16[96,1536]{1,0:T(8,128)(2,1)}, bf16[96,1536]{1,0:T(8,128)(2,1)S(1)}, u32[]{:S(2)}, u32[]{:S(2)}) collective-permute-start(bf16[96,1536]{1,0:T(8,128)(2,1)} %collective-permute-done.13), channel_id=1, source_target_pairs={{0,15},{1,0},{2,1},{3,2},{4,3},{5,4},{6,5},{7,6},{8,7},{9,8},{10,9... | collective-permute-start | bytes 884744 | tf_op jit(solution)/shard_map/ppermute | solution.py:19
  141.4 74.9 %copy-start.4 = (f32[64,16,96]{2,0,1:T(8,128)S(1)}, f32[64,16,96]{2,0,1:T(8,128)}, u32[]{:S(2)}) copy-start(f32[64,16,96]{2,0,1:T(8,128)} %all-reduce.3.cloned.1.call-done) | copy-start | bytes 1179652
  230.6 104.8 %copy-start.6 = (f32[16,64,64]{1,2,0:T(8,128)S(1)}, f32[16,64,64]{1,2,0:T(8,128)}, u32[]{:S(2)}) copy-start(f32[16,64,64]{1,2,0:T(8,128)} %copy-done.5) | copy-start | bytes 786436
  236.7 101.6 %copy-start.25 = (bf16[1536,96]{0,1:T(8,128)(2,1)S(1)}, bf16[1536,96]{0,1:T(8,128)(2,1)}, u32[]{:S(2)}) copy-start(bf16[1536,96]{0,1:T(8,128)(2,1)} %param.18) | copy-start | bytes 884740
  236.7 124.7 %copy-start.3 = (bf16[64,1536]{1,0:T(8,128)(2,1)S(1)}, bf16[64,1536]{1,0:T(8,128)(2,1)}, u32[]{:S(2)}) copy-start(bf16[64,1536]{1,0:T(8,128)(2,1)} %param.13) | copy-start | bytes 589828
  236.7 125.5 %copy-start.1 = (bf16[96,1536]{1,0:T(8,128)(2,1)S(1)}, bf16[96,1536]{1,0:T(8,128)(2,1)}, u32[]{:S(2)}) copy-start(bf16[96,1536]{1,0:T(8,128)(2,1)} %param.15) | copy-start | bytes 884740
  (14 other events, 198.0 us)
Sparse Core Ops, SparseCore 0:
  45.8 95.6 all-reduce.2
  143.7 54.5 all-gather.2
  248.1 87.2 all-reduce.4
